TPU v7x, 32 devices: a whole 2x2x4 slice. The times are simulated.
32 devices in a mesh: gy: 8 (over y, x, core), gz: 4 (over z).
Axes of the slice: x: 2, y: 2, z: 4, core: 2. Of those that a mesh axis runs over, the one named last changes fastest.
Arguments:
- dual_flow_speeds: float32 [3, 64, 64, 1024], P(None, 'gy', 'gz'), may hold values from -6 to 6
- dual_thermal_state: float32 [64, 64, 1024], P('gy', 'gz'), may hold values from -6 to 6
- forward_flow_speeds: bfloat16 [3, 64, 64, 1024], P(None, 'gy', 'gz'), may hold values from -4 to 4
- forward_thermal_state: bfloat16 [64, 64, 1024], P('gy', 'gz'), may hold values from -6 to 6
Outputs:
- advanced_dual_motion: float32 [3, 64, 64, 1024], P(None, 'gy', 'gz')
- advanced_dual_thermal: float32 [64, 64, 1024], P('gy', 'gz')
All inputs are finite; a program needn't handle non-finite values.
Results may differ from a plain program's by a relative error of at most 0.0003.
Values sent between devices are 32-bit elements; how exact they have to be, the bound alone decides.
A program may use at most 128 MiB of HBM per device.

v0:
```python
import functools
import math

import jax
import jax.numpy as jnp
import ml_dtypes
import numpy as np
from jax import lax
from jax.experimental import pallas as pl
from jax.experimental.pallas import tpu as pltpu
from jax.sharding import PartitionSpec as P

time_step = 0.2
viscosity = 0.1
diffusivity = 0.1
buoyancy = 1.0
highest = lax.Precision.HIGHEST


def padded(cells, sides, width):
    for axis, dim in sides:
        count = lax.axis_size(axis)
        head = lax.slice_in_dim(cells, 0, width, axis=dim)
        tail = lax.slice_in_dim(cells, cells.shape[dim] - width, cells.shape[dim], axis=dim)
        cells = jnp.concatenate(
            [
                lax.ppermute(tail, axis, [(i, (i + 1) % count) for i in range(count)]),
                cells,
                lax.ppermute(head, axis, [((i + 1) % count, i) for i in range(count)]),
            ],
            axis=dim,
        )
    return cells


def shifted(value, axis, by):
    length = lax.axis_size(axis)
    return lax.ppermute(value, axis, [(i, (i + by) % length) for i in range(length)])


def from_behind(block, axis, distance):
    devices = range(lax.axis_size(axis))
    route = [(i - distance, i) for i in devices if i - distance in devices]
    return lax.ppermute(block, axis, route)


def tendency_contributions(haloed_quantities, motion_pieces):
    centre = haloed_quantities[:, 1:-1, 1:-1]
    slope_x = 0.5 * (jnp.roll(centre, -1, axis=3) - jnp.roll(centre, 1, axis=3))
    slope_y = 0.5 * (haloed_quantities[:, 2:, 1:-1] - haloed_quantities[:, :-2, 1:-1])
    slope_z = 0.5 * (haloed_quantities[:, 1:-1, 2:] - haloed_quantities[:, 1:-1, :-2])
    laplace = (
        jnp.roll(centre[:4], -1, axis=3)
        + jnp.roll(centre[:4], 1, axis=3)
        + (haloed_quantities[:4, 2:, 1:-1] + haloed_quantities[:4, :-2, 1:-1])
        + (haloed_quantities[:4, 1:-1, 2:] + haloed_quantities[:4, 1:-1, :-2])
        - 6.0 * centre[:4]
    )
    advect = (
        motion_pieces[0] * slope_x[:4]
        + motion_pieces[1] * slope_y[:4]
        + motion_pieces[2] * slope_z[:4]
    )
    heat_slope = jnp.stack([slope_x[4], slope_y[4], slope_z[4]])
    unprojected_motion = centre[:3] + time_step * (
        advect[:3] + viscosity * laplace[:3] + centre[3] * heat_slope
    )
    thermal_following = centre[3] + time_step * (
        advect[3] + diffusivity * laplace[3] + buoyancy * centre[2]
    )
    return (unprojected_motion, thermal_following)


def cas_table(length):
    indices = jnp.arange(length, dtype=jnp.int32)
    phases = indices[:, None] * indices[None, :] % length
    angles = phases.astype(jnp.float32) * (2.0 * math.pi / length)
    return jnp.cos(angles) + jnp.sin(angles)


def cosine_table(length):
    indices = jnp.arange(length, dtype=jnp.int32)
    phases = indices[None, :] * (2 * indices[:, None] + 1) % (4 * length)
    return jnp.cos(phases.astype(jnp.float32) * (math.pi / (2 * length)))


def cosine_inverse(length):
    indices = jnp.arange(length, dtype=jnp.int32)
    weights = jnp.where(indices == 0, 1.0, 2.0).astype(jnp.float32)
    return cosine_table(length).T * weights[:, None] / length


def eigen_periodic(waves, length):
    return 2.0 - 2.0 * jnp.cos(waves.astype(jnp.float32) * (2.0 * math.pi / length))


def eigen_wall(waves, length):
    return 2.0 - 2.0 * jnp.cos(waves.astype(jnp.float32) * (math.pi / length))


def invert(spectral, eigen_sum):
    positive = eigen_sum > 0
    return jnp.where(positive, -spectral / jnp.where(positive, eigen_sum, 1.0), 0.0)


def wall_mask(extent, margin, position, groups):
    layer_index = jnp.arange(extent, dtype=jnp.int32)
    bottom = (layer_index < margin) & (position == 0)
    ceiling = (layer_index >= extent - margin) & (position == groups - 1)
    return jnp.where(bottom | ceiling, 0.0, 1.0).astype(jnp.float32)


def poisson(source):
    spanwise_extent, vertical_extent, lengthwise_extent = source.shape
    groups_y = lax.axis_size("gy")
    groups_z = lax.axis_size("gz")
    span_y = spanwise_extent * groups_y
    span_z = vertical_extent * groups_z
    hart_x = cas_table(lengthwise_extent)
    hart_y = cas_table(span_y)
    cos_forward = cosine_table(span_z).reshape(groups_z, vertical_extent, span_z)
    cos_backward = cosine_inverse(span_z).reshape(span_z, groups_z, vertical_extent)
    line_z = eigen_wall(jnp.arange(span_z, dtype=jnp.int32), span_z)
    piece_x = lengthwise_extent // groups_y
    quarter = span_y // groups_z
    table_x = hart_x.reshape(lengthwise_extent, groups_y, piece_x)
    table_y = hart_y.reshape(groups_y, spanwise_extent, groups_z, quarter)
    step_one = jnp.einsum("yzx,xgj->gjyz", source, table_x, precision=highest).reshape(groups_y, -1)
    step_one = lax.all_to_all(step_one, "gy", split_axis=0, concat_axis=0, tiled=True).reshape(
        groups_y, piece_x, spanwise_extent, vertical_extent
    )
    step_two = jnp.einsum("sjyz,syhq->hjqz", step_one, table_y, precision=highest).reshape(
        groups_z, -1
    )
    step_two = lax.all_to_all(step_two, "gz", split_axis=0, concat_axis=0, tiled=True).reshape(
        groups_z, piece_x, quarter, vertical_extent
    )
    spectral = jnp.einsum("tjqc,tck->jqk", step_two, cos_forward, precision=highest)
    wave_x = lax.axis_index("gy") * piece_x + jnp.arange(piece_x, dtype=jnp.int32)
    wave_y = lax.axis_index("gz") * quarter + jnp.arange(quarter, dtype=jnp.int32)
    eigen_sum = (
        eigen_periodic(wave_x, lengthwise_extent)[:, None, None]
        + eigen_periodic(wave_y, span_y)[None, :, None]
        + line_z[None, None, :]
    )
    solved = invert(spectral, eigen_sum)
    step_three = jnp.einsum("jqk,ktc->tjqc", solved, cos_backward, precision=highest).reshape(
        groups_z, -1
    )
    step_three = lax.all_to_all(step_three, "gz", split_axis=0, concat_axis=0, tiled=True).reshape(
        groups_z, piece_x, quarter, vertical_extent
    )
    step_four = (
        jnp.einsum("hjqz,syhq->sjyz", step_three, table_y, precision=highest) * (1.0 / span_y)
    ).reshape(groups_y, -1)
    step_four = lax.all_to_all(step_four, "gy", split_axis=0, concat_axis=0, tiled=True).reshape(
        groups_y, piece_x, spanwise_extent, vertical_extent
    )
    return jnp.einsum("gjyz,xgj->yzx", step_four, table_x, precision=highest) * (
        1.0 / lengthwise_extent
    )


def on_device(dual_flow_speeds, dual_thermal_state, forward_flow_speeds, forward_thermal_state):
    spanwise_extent, vertical_extent, lengthwise_extent = dual_thermal_state.shape
    groups_z = lax.axis_size("gz")
    place_z = lax.axis_index("gz")
    motion_pieces = forward_flow_speeds.astype(jnp.float32)
    forward_thermal_flux = forward_thermal_state.astype(jnp.float32)
    stacked_fields = jnp.concatenate(
        [dual_flow_speeds, dual_thermal_state[None], forward_thermal_flux[None]], 0
    )
    haloed_quantities = padded(stacked_fields, (("gy", 1), ("gz", 2)), 1)
    haloed_quantities = (
        haloed_quantities
        * wall_mask(vertical_extent + 2, 1, place_z, groups_z)[None, None, :, None]
    )
    unprojected_motion, advanced_dual_thermal = tendency_contributions(
        haloed_quantities, motion_pieces
    )
    upper_y = shifted(unprojected_motion[1][0], "gy", -1)
    upper_z = from_behind(unprojected_motion[2][:, 0], "gz", -1)
    next_y = jnp.concatenate([unprojected_motion[1][1:], upper_y[None]], 0)
    next_z = jnp.concatenate([unprojected_motion[2][:, 1:], upper_z[:, None]], 1)
    source = (
        jnp.roll(unprojected_motion[0], -1, axis=2)
        - unprojected_motion[0]
        + (next_y - unprojected_motion[1])
        + (next_z - unprojected_motion[2])
    )
    pressure = poisson(source)
    grad_x = pressure - jnp.roll(pressure, 1, axis=2)
    lower_y = shifted(pressure[spanwise_extent - 1], "gy", 1)
    grad_y = pressure - jnp.concatenate([lower_y[None], pressure[:-1]], 0)
    lower_z = from_behind(pressure[:, vertical_extent - 1], "gz", 1)
    below = jnp.concatenate([lower_z[:, None], pressure[:, :-1]], 1)
    floor_layer = (jnp.arange(vertical_extent, dtype=jnp.int32) == 0) & (place_z == 0)
    grad_z = jnp.where(floor_layer[None, :, None], 0.0, pressure - below)
    advanced_dual_motion = unprojected_motion - jnp.stack([grad_x, grad_y, grad_z])
    return (advanced_dual_motion, advanced_dual_thermal)


def halves(table):
    high = table.astype(np.float32).astype(ml_dtypes.bfloat16)
    low = (table - high.astype(np.float64)).astype(np.float32).astype(ml_dtypes.bfloat16)
    return high, low


def cas_np(length):
    phases = np.outer(np.arange(length), np.arange(length)) % length
    angles = phases * (2.0 * np.pi / length)
    return np.cos(angles) + np.sin(angles)


@functools.lru_cache(maxsize=None)
def tables(length, span_y, span_z, groups_y, groups_z):
    hart_x = cas_np(length)
    chunks = groups_y // 2
    hx = [
        np.ascontiguousarray(t.reshape(length, chunks, length // chunks).transpose(1, 0, 2))
        for t in halves(hart_x)
    ]
    hart_y = cas_np(span_y)
    forward = halves(hart_y * (-1.0 / (span_y * length)))
    backward = halves(hart_y)
    ty = np.stack([np.concatenate([hi, hi, lo], 1) for hi, lo in (forward, backward)])
    line_x = 4.0 * np.sin(np.pi * np.arange(length) / length) ** 2
    line_y = 4.0 * np.sin(np.pi * np.arange(span_y) / span_y) ** 2
    modes = (line_x[None, :] + line_y[:, None]).astype(np.float32)
    modes = np.ascontiguousarray(modes.reshape(span_y, groups_y, -1).transpose(1, 0, 2))
    k = np.arange(span_z)
    basis = np.cos(np.pi * np.outer(k, 2 * k + 1) / (2 * span_z))
    eig = 4.0 * np.sin(np.pi * k / (2 * span_z)) ** 2
    scale = np.where(k == 0, 0.0, 2.0 / (span_z * np.where(k == 0, 1.0, eig)))
    mean_free = (basis.T * scale) @ basis
    mean_free = mean_free.astype(np.float32).reshape(groups_z, -1, span_z)
    return hx[0], hx[1], ty, modes, mean_free


def split_rows(value):
    high = value.astype(jnp.bfloat16)
    return high, (value - high.astype(jnp.float32)).astype(jnp.bfloat16)


def dot32(a, b):
    return jnp.dot(a, b, preferred_element_type=jnp.float32)


def fused_kernel(
    ny, nz, motion, thermal, flow, base, hx_hi, hx_lo, ty_in, modes_in, free_in,
    out_motion, out_thermal,
    F, U, TH, HH, HL, TY, LAM, FREE, ZS, ZR, P0, P1, P2, PZS, PZR, S, A, B, D, PHI,
    R, MSG, MR, A2, B2, PR, QZS, QZR, OM, OT, lsem, osem, hs, hr, as_, ar, bs, br, zs, zr,
):
    gy, gz = lax.axis_index("gy"), lax.axis_index("gz")
    rows, layers, length = thermal.shape
    mesh_id = pl.DeviceIdType.MESH
    up_y, down_y = (gy + 1) % ny, (gy + ny - 1) % ny
    has_up, has_down = gz < nz - 1, gz > 0

    loads = [
        pltpu.make_async_copy(motion, F.at[0:3, 1 : rows + 1], lsem.at[0]),
        pltpu.make_async_copy(thermal, F.at[3, 1 : rows + 1], lsem.at[1]),
        pltpu.make_async_copy(base, TH, lsem.at[2]),
        pltpu.make_async_copy(flow, U, lsem.at[3]),
        pltpu.make_async_copy(modes_in.at[gy], LAM, lsem.at[4]),
        pltpu.make_async_copy(free_in.at[gz], FREE, lsem.at[5]),
        pltpu.make_async_copy(ty_in, TY, lsem.at[6]),
        pltpu.make_async_copy(hx_hi, HH, lsem.at[7]),
        pltpu.make_async_copy(hx_lo, HL, lsem.at[8]),
    ]
    for copy in loads:
        copy.start()

    barrier = pltpu.get_barrier_semaphore()
    for i in range(1, ny):
        pl.semaphore_signal(
            barrier, inc=1, device_id=((gy + i) % ny, gz), device_id_type=mesh_id
        )
    for i in range(1, nz):
        pl.semaphore_signal(
            barrier, inc=1, device_id=(gy, (gz + i) % nz), device_id_type=mesh_id
        )

    def remote(src, dst, ssem, rsem, y, z):
        return pltpu.make_async_remote_copy(
            src_ref=src, dst_ref=dst, send_sem=ssem, recv_sem=rsem,
            device_id=(y, z), device_id_type=mesh_id,
        )

    loads[2].wait()
    for y in range(rows):
        F[4, y + 1] = TH[y].astype(jnp.float32)
    loads[0].wait()
    loads[1].wait()
    for f in range(5):
        for y in range(rows):
            ZS[0, f, y : y + 1, :] = F[f, y + 1, 0:1, :]
            ZS[1, f, y : y + 1, :] = F[f, y + 1, layers - 1 : layers, :]
    pl.semaphore_wait(barrier, ny + nz - 2)

    z_down = remote(ZS.at[0], ZR.at[1], hs.at[0], hr.at[0], gy, gz - 1)
    z_up = remote(ZS.at[1], ZR.at[0], hs.at[1], hr.at[1], gy, gz + 1)
    y_down = remote(F.at[:, 1], F.at[:, rows + 1], hs.at[2], hr.at[2], down_y, gz)
    y_up = remote(F.at[:, rows], F.at[:, 0], hs.at[3], hr.at[3], up_y, gz)

    @pl.when(has_down)
    def _():
        z_down.start()

    @pl.when(has_up)
    def _():
        z_up.start()

    y_down.start()
    y_up.start()

    @pl.when(gz == 0)
    def _():
        ZR[0] = jnp.zeros_like(ZR[0])

    @pl.when(gz == nz - 1)
    def _():
        ZR[1] = jnp.zeros_like(ZR[1])
        PZR[...] = jnp.zeros_like(PZR)

    loads[4].wait()
    D[0] = jnp.zeros_like(D[0])

    def ratios(block, carry):
        def one(i, prod):
            at = block * layers + i
            e = LAM[...] + D[at]
            d = e / (1.0 + e)
            D[at + 1] = d
            return prod * (1.0 - d)

        PHI[block] = lax.fori_loop(0, layers, one, jnp.ones_like(LAM[...]))
        return carry

    lax.fori_loop(0, nz, ratios, 0)

    loads[3].wait()

    @pl.when(has_up)
    def _():
        z_down.wait_recv()

    @pl.when(has_down)
    def _():
        z_up.wait_recv()

    y_down.wait_recv()
    y_up.wait_recv()

    zi = lax.broadcasted_iota(jnp.int32, (layers, length), 0)

    def stencil(y, carry):
        def sides(f):
            c = F[f, y + 1]
            xp, xm = pltpu.roll(c, length - 1, 1), pltpu.roll(c, 1, 1)
            zp = jnp.where(zi == layers - 1, ZR[1, f, pl.ds(y, 1), :], pltpu.roll(c, layers - 1, 0))
            zm = jnp.where(zi == 0, ZR[0, f, pl.ds(y, 1), :], pltpu.roll(c, 1, 0))
            return c, xp, xm, F[f, y + 2], F[f, y], zp, zm

        u0, u1, u2 = (U[d, y].astype(jnp.float32) for d in range(3))

        def advance(f):
            c, xp, xm, yp, ym, zp, zm = sides(f)
            adv = 0.5 * (u0 * (xp - xm) + u1 * (yp - ym) + u2 * (zp - zm))
            lap = (xp + xm) + (yp + ym) + (zp + zm) - 6.0 * c
            return c, adv + viscosity * lap

        c3, t3 = advance(3)
        _, hxp, hxm, hyp, hym, hzp, hzm = sides(4)
        half = 0.5 * c3
        c, t = advance(0)
        P0[y] = c + time_step * (t + half * (hxp - hxm))
        c, t = advance(1)
        P1[y] = c + time_step * (t + half * (hyp - hym))
        c, t = advance(2)
        p2 = c + time_step * (t + half * (hzp - hzm))
        P2[y] = p2
        PZS[pl.ds(y, 1), :] = p2[0:1, :]
        OT[y] = c3 + time_step * (t3 + buoyancy * c)
        return carry

    p1_down = remote(P1.at[0], P1.at[rows], hs.at[4], hr.at[4], down_y, gz)
    p2_down = remote(PZS, PZR, hs.at[5], hr.at[5], gy, gz - 1)
    stencil(0, 0)
    p1_down.start()
    lax.fori_loop(1, rows, stencil, 0)

    @pl.when(has_down)
    def _():
        p2_down.start()

    out_t = pltpu.make_async_copy(OT, out_thermal, osem.at[0])
    out_t.start()

    @pl.when(has_up)
    def _():
        p2_down.wait_recv()

    p1_down.wait_recv()
    half_rows = rows * layers

    def diverge(y, carry):
        p0, p2 = P0[y], P2[y]
        zp = jnp.where(zi == layers - 1, PZR[pl.ds(y, 1), :], pltpu.roll(p2, layers - 1, 0))
        s = (pltpu.roll(p0, length - 1, 1) - p0) + (P1[y + 1] - P1[y]) + (zp - p2)
        high, low = split_rows(s)
        S[pl.ds(pl.multiple_of(y * layers, layers), layers), :] = high
        S[pl.ds(pl.multiple_of(half_rows + y * layers, layers), layers), :] = low
        return carry

    lax.fori_loop(0, rows, diverge, 0)

    loads[7].wait()
    loads[8].wait()
    chunks = ny // 2

    def x_forward(i, carry):
        c = (gy // 2 + 1 + i) % chunks
        wide = dot32(S[...], HH[c])
        part = wide[:half_rows] + wide[half_rows:] + dot32(S[0:half_rows, :], HL[c])
        for side in range(2):
            peer = 2 * c + side
            A[peer] = part[:, side * 128 : (side + 1) * 128]

            @pl.when(peer != gy)
            def _():
                remote(A.at[peer], B.at[gy], as_.at[peer], ar.at[gy], peer, gz).start()

            @pl.when(peer == gy)
            def _():
                B[peer] = A[peer]

        return carry

    lax.fori_loop(0, chunks, x_forward, 0)
    loads[5].wait()
    loads[6].wait()

    def wait_all(src, dst, ssem, rsem):
        def one(i, carry):
            peer = (gy + i) % ny
            remote(src.at[peer], dst.at[peer], ssem.at[peer], rsem.at[peer], peer, gz).wait_recv()
            return carry

        lax.fori_loop(1, ny, one, 0)

    wait_all(A, B, as_, ar)
    span_y = ny * rows
    flat = B.reshape(ny * half_rows, 128)

    def y_transform(pair, table):
        high, low = split_rows(pair)
        return dot32(table, jnp.concatenate([high, low, high], 0))

    f_sweep = None
    start = gz * layers
    total = nz * layers
    for z in range(0, layers, 2):
        pair = jnp.concatenate(
            [flat[pl.ds(z + k, span_y, stride=layers), :] for k in range(2)], 1
        )
        res = y_transform(pair, TY[0])
        for k in range(2):
            r = res[:, k * 128 : (k + 1) * 128]
            R[z + k] = r
            MSG[0, span_y + z + k : span_y + z + k + 1, :] = r[0:1, :]
            MSG[1, span_y + z + k : span_y + z + k + 1, :] = r[0:1, :]
            w = 1.0 - D[start + z + k + 1]
            f_sweep = w * (r if f_sweep is None else r + f_sweep)
    MSG[0, 0:span_y, :] = f_sweep
    g_sweep = jnp.zeros_like(f_sweep)
    for z in range(layers - 1, -1, -1):
        g_sweep = (1.0 - D[total - start - z]) * (R[z] + g_sweep)
    MSG[1, 0:span_y, :] = g_sweep

    for i in range(1, nz):
        peer = (gz + i) % nz

        @pl.when(peer > gz)
        def _():
            remote(MSG.at[0], MR.at[gz], zs.at[peer], zr.at[gz], gy, peer).start()

        @pl.when(peer < gz)
        def _():
            remote(MSG.at[1], MR.at[gz], zs.at[peer], zr.at[gz], gy, peer).start()

    MR[gz] = MSG[0]
    for i in range(1, nz):
        peer = (gz + i) % nz
        remote(MSG.at[0], MR.at[peer], zs.at[peer], zr.at[peer], gy, peer).wait_recv()

    f = jnp.zeros_like(f_sweep)
    g = jnp.zeros_like(f_sweep)
    for s in range(nz):
        f = jnp.where(s < gz, MR[s, 0:span_y, :] + PHI[s] * f, f)
    for s in range(nz - 1, -1, -1):
        g = jnp.where(s > gz, MR[s, 0:span_y, :] + PHI[nz - 1 - s] * g, g)
    line = jnp.concatenate([MR[s, span_y:, :] for s in range(nz)], 0)
    level = jnp.dot(FREE[...], line, precision=highest, preferred_element_type=jnp.float32)
    plain = LAM[...] > 0.0
    for z in range(layers):
        f = (1.0 - D[start + z + 1]) * (R[z] + f)
        R[z] = f
    d_low, d_high = D[start + layers], D[total - start - layers]
    below = d_low + d_high - d_low * d_high
    p = (f + (1.0 - d_low) * g) / jnp.where(plain, below, 1.0)
    R[layers - 1] = p
    for z in range(layers - 2, -1, -1):
        p = (1.0 - D[start + z + 1]) * p + R[z]
        R[z] = p
    flat2 = A2.reshape(ny * half_rows, 128)
    for z in range(0, layers, 2):
        pair = jnp.concatenate(
            [jnp.where(plain, R[z + k], level[z + k : z + k + 1, :]) for k in range(2)], 1
        )
        res = y_transform(pair, TY[1])
        for k in range(2):
            flat2[pl.ds(z + k, span_y, stride=layers), :] = res[:, k * 128 : (k + 1) * 128]

    def send_back(i, carry):
        peer = (gy + i) % ny
        remote(A2.at[peer], B2.at[gy], bs.at[peer], br.at[gy], peer, gz).start()
        return carry

    lax.fori_loop(1, ny, send_back, 0)
    B2[gy] = A2[gy]
    wait_all(A2, B2, bs, br)

    q = jnp.concatenate([B2[s] for s in range(ny)], 1)
    high, low = split_rows(q)
    S[0:half_rows, :] = high
    S[half_rows:, :] = low
    width = length // chunks
    for c in range(chunks):
        wide = dot32(S[...], HH[c])
        part = wide[:half_rows] + wide[half_rows:] + dot32(S[0:half_rows, :], HL[c])
        PR[1 : rows + 1, :, c * width : (c + 1) * width] = part.reshape(rows, layers, width)
    pr_up = remote(PR.at[rows], PR.at[0], hs.at[6], hr.at[6], up_y, gz)
    pz_up = remote(QZS, QZR, hs.at[7], hr.at[7], gy, gz + 1)
    pr_up.start()
    for y in range(rows):
        QZS[y : y + 1, :] = PR[y + 1, layers - 1 : layers, :]

    @pl.when(has_up)
    def _():
        pz_up.start()

    @pl.when(gz == 0)
    def _():
        for y in range(rows):
            QZR[y : y + 1, :] = PR[y + 1, 0:1, :]

    @pl.when(has_down)
    def _():
        pz_up.wait_recv()

    pr_up.wait_recv()

    def project(y, carry):
        p = PR[y + 1]
        zm = jnp.where(zi == 0, QZR[pl.ds(y, 1), :], pltpu.roll(p, 1, 0))
        OM[0, y] = P0[y] - (p - pltpu.roll(p, 1, 1))
        OM[1, y] = P1[y] - (p - PR[y])
        OM[2, y] = P2[y] - (p - zm)
        return carry

    lax.fori_loop(0, rows, project, 0)
    out_m = pltpu.make_async_copy(OM, out_motion, osem.at[1])
    out_m.start()

    @pl.when(has_down)
    def _():
        z_down.wait_send()
        p2_down.wait_send()

    @pl.when(has_up)
    def _():
        z_up.wait_send()
        pz_up.wait_send()

    for copy in (y_down, y_up, p1_down, pr_up):
        copy.wait_send()

    def finish(i, carry):
        peer = (gy + i) % ny
        remote(A.at[peer], B.at[gy], as_.at[peer], ar.at[gy], peer, gz).wait_send()
        remote(A2.at[peer], B2.at[gy], bs.at[peer], br.at[gy], peer, gz).wait_send()
        return carry

    lax.fori_loop(1, ny, finish, 0)
    for i in range(1, nz):
        peer = (gz + i) % nz
        remote(MSG.at[0], MR.at[gz], zs.at[peer], zr.at[gz], gy, peer).wait_send()
    out_t.wait()
    out_m.wait()


def fused_step(ny, nz, motion, thermal, flow, base):
    rows, layers, length = thermal.shape
    span_y, span_z = ny * rows, nz * layers
    constants = [jnp.asarray(t) for t in tables(length, span_y, span_z, ny, nz)]
    f32, b16 = jnp.float32, jnp.bfloat16
    flat = rows * layers
    vmem, dma = pltpu.VMEM, pltpu.SemaphoreType.DMA
    scratch = [
        vmem((5, rows + 2, layers, length), f32),
        vmem(flow.shape, b16),
        vmem(base.shape, b16),
        vmem(constants[0].shape, b16),
        vmem(constants[1].shape, b16),
        vmem(constants[2].shape, b16),
        vmem((span_y, 128), f32),
        vmem((layers, span_z), f32),
        vmem((2, 5, rows, length), f32),
        vmem((2, 5, rows, length), f32),
        vmem((rows, layers, length), f32),
        vmem((rows + 1, layers, length), f32),
        vmem((rows, layers, length), f32),
        vmem((rows, length), f32),
        vmem((rows, length), f32),
        vmem((2 * flat, length), b16),
        vmem((ny, flat, 128), f32),
        vmem((ny, flat, 128), f32),
        vmem((span_z + 1, span_y, 128), f32),
        vmem((nz, span_y, 128), f32),
        vmem((layers, span_y, 128), f32),
        vmem((2, span_y + layers, 128), f32),
        vmem((nz, span_y + layers, 128), f32),
        vmem((ny, flat, 128), f32),
        vmem((ny, flat, 128), f32),
        vmem((rows + 1, layers, length), f32),
        vmem((rows, length), f32),
        vmem((rows, length), f32),
        vmem((3, rows, layers, length), f32),
        vmem((rows, layers, length), f32),
        dma((9,)),
        dma((2,)),
        dma((8,)),
        dma((8,)),
        dma((ny,)),
        dma((ny,)),
        dma((ny,)),
        dma((ny,)),
        dma((nz,)),
        dma((nz,)),
    ]
    hbm = pl.BlockSpec(memory_space=pl.ANY)
    return pl.pallas_call(
        functools.partial(fused_kernel, ny, nz),
        out_shape=(
            jax.ShapeDtypeStruct(motion.shape, f32),
            jax.ShapeDtypeStruct(thermal.shape, f32),
        ),
        in_specs=[hbm] * 9,
        out_specs=(hbm, hbm),
        scratch_shapes=scratch,
        compiler_params=pltpu.CompilerParams(
            collective_id=0, has_side_effects=True, vmem_limit_bytes=44 * 2**20
        ),
        cost_estimate=pl.CostEstimate(
            flops=12 * flat * length * length, bytes_accessed=10 * 2**20, transcendentals=0
        ),
    )(motion, thermal, flow, base, *constants)


def solution(mesh):
    placed = (
        P(None, "gy", "gz", None),
        P("gy", "gz", None),
        P(None, "gy", "gz", None),
        P("gy", "gz", None),
    )
    groups_y, groups_z = mesh.shape["gy"], mesh.shape["gz"]

    def step(motion, thermal, flow, base):
        rows, layers, length = thermal.shape
        if length == 128 * groups_y and groups_y % 2 == 0 and rows == 8 and layers == 16:
            return fused_step(groups_y, groups_z, motion, thermal, flow, base)
        return on_device(motion, thermal, flow, base)

    return jax.shard_map(
        step,
        mesh=mesh,
        in_specs=placed,
        out_specs=(P(None, "gy", "gz", None), P("gy", "gz", None)),
        check_vma=False,
    )
```

profile of v0, /device:TPU:0, one launch (start us, length us, event | category | flops | bytes accessed | tf_op | source)
XLA Modules:
  0.0 59.1 jit_solution(4193860671293134696)
XLA Ops:
  0.6 0.0 copy-start
  0.6 1.6 %copy-done = bf16[4,1024,256]{2,1,0:T(8,128)(2,1)S(1)} copy-done((bf16[4,1024,256]{2,1,0:T(8,128)(2,1)S(1)}, bf16[4,1024,256]{2,1,0:T(8,128)(2,1)}, u32[]{:S(2)}) %copy-start) | copy-done | bytes 2097176
  2.2 0.0 copy-start.1
  2.2 1.6 %copy-done.1 = bf16[4,1024,256]{2,1,0:T(8,128)(2,1)S(1)} copy-done((bf16[4,1024,256]{2,1,0:T(8,128)(2,1)S(1)}, bf16[4,1024,256]{2,1,0:T(8,128)(2,1)}, u32[]{:S(2)}) %copy-start.1) | copy-done | bytes 2097176
  3.8 0.0 copy-start.2
  3.8 1.4 %copy-done.2 = f32[3,8,16,1024]{3,2,1,0:T(8,128)S(1)} copy-done((f32[3,8,16,1024]{3,2,1,0:T(8,128)S(1)}, f32[3,8,16,1024]{3,2,1,0:T(8,128)}, u32[]{:S(2)}) %copy-start.2) | copy-done | bytes 1572888
  5.2 0.0 copy-start.3
  5.2 1.1 %copy-done.3 = bf16[3,8,16,1024]{3,2,1,0:T(8,128)(2,1)S(1)} copy-done((bf16[3,8,16,1024]{3,2,1,0:T(8,128)(2,1)S(1)}, bf16[3,8,16,1024]{3,2,1,0:T(8,128)(2,1)}, u32[]{:S(2)}) %copy-start.3) | copy-done | bytes 786456
  6.4 0.0 copy-start.4
  6.4 1.0 %copy-done.4 = f32[8,16,1024]{2,1,0:T(8,128)S(1)} copy-done((f32[8,16,1024]{2,1,0:T(8,128)S(1)}, f32[8,16,1024]{2,1,0:T(8,128)}, u32[]{:S(2)}) %copy-start.4) | copy-done | bytes 524312
  7.4 0.0 copy-start.5
  7.4 0.9 %copy-done.5 = bf16[8,16,1024]{2,1,0:T(8,128)(2,1)S(1)} copy-done((bf16[8,16,1024]{2,1,0:T(8,128)(2,1)S(1)}, bf16[8,16,1024]{2,1,0:T(8,128)(2,1)}, u32[]{:S(2)}) %copy-start.5) | copy-done | bytes 262168
  8.4 0.0 copy-start.6
  8.4 0.9 %copy-done.6 = f32[8,64,128]{2,1,0:T(8,128)S(1)} copy-done((f32[8,64,128]{2,1,0:T(8,128)S(1)}, f32[8,64,128]{2,1,0:T(8,128)}, u32[]{:S(2)}) %copy-start.6) | copy-done | bytes 262168
  9.3 0.0 copy-start.7
  9.3 0.8 %copy-done.7 = bf16[2,64,192]{2,1,0:T(8,128)(2,1)S(1)} copy-done((bf16[2,64,192]{2,1,0:T(8,128)(2,1)S(1)}, bf16[2,64,192]{2,1,0:T(8,128)(2,1)}, u32[]{:S(2)}) %copy-start.7) | copy-done | bytes 49176
  10.1 0.0 copy-start.8
  10.1 0.8 %copy-done.8 = f32[4,16,64]{2,1,0:T(8,128)S(1)} copy-done((f32[4,16,64]{2,1,0:T(8,128)S(1)}, f32[4,16,64]{2,1,0:T(8,128)}, u32[]{:S(2)}) %copy-start.8) | copy-done | bytes 16408
  10.9 46.3 %shard_map.104 = (f32[3,8,16,1024]{3,2,1,0:T(8,128)S(1)}, f32[8,16,1024]{2,1,0:T(8,128)S(1)}) custom-call(f32[3,8,16,1024]{3,2,1,0:T(8,128)S(1)} %copy-done.2, f32[8,16,1024]{2,1,0:T(8,128)S(1)} %copy-done.4, bf16[3,8,16,1024]{3,2,1,0:T(8,128)(2,1)S(1)} %copy-done.3, bf16[8,16,1024]{2,1,0:T(8,128)(2,1)S(1)} %copy-done.5, ...), custom_call_target="tpu_custom_call" | custom-call | flops 1610612736 | bytes 10485760 | tf_op jit(solution)/shard_map/pallas_call | solution.py:654
  57.2 1.1 %copy.13 = f32[3,8,16,1024]{3,2,1,0:T(8,128)} copy(f32[3,8,16,1024]{3,2,1,0:T(8,128)S(1)} %get-tuple-element.4) | data formatting | bytes 3145728
  58.3 0.8 %copy.14 = f32[8,16,1024]{2,1,0:T(8,128)} copy(f32[8,16,1024]{2,1,0:T(8,128)S(1)} %get-tuple-element.5) | data formatting | bytes 1048576
Async XLA Ops:
  0.6 1.6 %copy-start = (bf16[4,1024,256]{2,1,0:T(8,128)(2,1)S(1)}, bf16[4,1024,256]{2,1,0:T(8,128)(2,1)}, u32[]{:S(2)}) copy-start(bf16[4,1024,256]{2,1,0:T(8,128)(2,1)} %constant.11.clone.hx_lo) | copy-start | bytes 6291460
  2.2 1.6 %copy-start.1 = (bf16[4,1024,256]{2,1,0:T(8,128)(2,1)S(1)}, bf16[4,1024,256]{2,1,0:T(8,128)(2,1)}, u32[]{:S(2)}) copy-start(bf16[4,1024,256]{2,1,0:T(8,128)(2,1)} %constant.10.clone.hx_hi) | copy-start | bytes 6291460
  3.8 1.4 %copy-start.2 = (f32[3,8,16,1024]{3,2,1,0:T(8,128)S(1)}, f32[3,8,16,1024]{3,2,1,0:T(8,128)}, u32[]{:S(2)}) copy-start(f32[3,8,16,1024]{3,2,1,0:T(8,128)} %motion.1) | copy-start | bytes 4718596
  5.2 1.1 %copy-start.3 = (bf16[3,8,16,1024]{3,2,1,0:T(8,128)(2,1)S(1)}, bf16[3,8,16,1024]{3,2,1,0:T(8,128)(2,1)}, u32[]{:S(2)}) copy-start(bf16[3,8,16,1024]{3,2,1,0:T(8,128)(2,1)} %flow.1) | copy-start | bytes 2359300
  6.4 1.0 %copy-start.4 = (f32[8,16,1024]{2,1,0:T(8,128)S(1)}, f32[8,16,1024]{2,1,0:T(8,128)}, u32[]{:S(2)}) copy-start(f32[8,16,1024]{2,1,0:T(8,128)} %thermal.1) | copy-start | bytes 1572868
  7.4 0.9 %copy-start.5 = (bf16[8,16,1024]{2,1,0:T(8,128)(2,1)S(1)}, bf16[8,16,1024]{2,1,0:T(8,128)(2,1)}, u32[]{:S(2)}) copy-start(bf16[8,16,1024]{2,1,0:T(8,128)(2,1)} %base.1) | copy-start | bytes 786436
  8.4 0.9 %copy-start.6 = (f32[8,64,128]{2,1,0:T(8,128)S(1)}, f32[8,64,128]{2,1,0:T(8,128)}, u32[]{:S(2)}) copy-start(f32[8,64,128]{2,1,0:T(8,128)} %constant.13.clone.modes_in) | copy-start | bytes 786436
  9.3 0.8 %copy-start.7 = (bf16[2,64,192]{2,1,0:T(8,128)(2,1)S(1)}, bf16[2,64,192]{2,1,0:T(8,128)(2,1)}, u32[]{:S(2)}) copy-start(bf16[2,64,192]{2,1,0:T(8,128)(2,1)} %constant.12.clone.ty_in) | copy-start | bytes 147460
  10.1 0.8 %copy-start.8 = (f32[4,16,64]{2,1,0:T(8,128)S(1)}, f32[4,16,64]{2,1,0:T(8,128)}, u32[]{:S(2)}) copy-start(f32[4,16,64]{2,1,0:T(8,128)} %constant.14.clone.free_in) | copy-start | bytes 49156
where the time goes:
time: 59.6 us; the launch traced here: 59.1 us
  Pallas kernels  46.3 us (78%)
  local copies, waits for them, and re-layouts  12.2 us (20%)
  between operations  0.66 us (1%)
    pallas_call x1, Pallas kernels, fused_step(): pl.pallas_call(functools.partial(fused_kernel, ny, nz), out_shape=(jax.Sh...  46.3 us
    unnamed x20, local copies, waits for them, and re-layouts  12.2 us

commit v1 on v0

--- a/solution.py
+++ b/solution.py
@@ -248,9 +248,9 @@
 
 def fused_kernel(
     ny, nz, motion, thermal, flow, base, hx_hi, hx_lo, ty_in, modes_in, free_in,
-    out_motion, out_thermal,
+    OM, OT,
     F, U, TH, HH, HL, TY, LAM, FREE, ZS, ZR, P0, P1, P2, PZS, PZR, S, A, B, D, PHI,
-    R, MSG, MR, A2, B2, PR, QZS, QZR, OM, OT, lsem, osem, hs, hr, as_, ar, bs, br, zs, zr,
+    R, MSG, MR, A2, B2, PR, QZS, QZR, lsem, hs, hr, as_, ar, bs, br, zs, zr,
 ):
     gy, gz = lax.axis_index("gy"), lax.axis_index("gz")
     rows, layers, length = thermal.shape
@@ -350,9 +350,6 @@
     def _():
         z_up.wait_recv()
 
-    y_down.wait_recv()
-    y_up.wait_recv()
-
     zi = lax.broadcasted_iota(jnp.int32, (layers, length), 0)
 
     def stencil(y, carry):
@@ -387,16 +384,16 @@
 
     p1_down = remote(P1.at[0], P1.at[rows], hs.at[4], hr.at[4], down_y, gz)
     p2_down = remote(PZS, PZR, hs.at[5], hr.at[5], gy, gz - 1)
+    lax.fori_loop(1, rows - 1, stencil, 0)
+    y_down.wait_recv()
+    y_up.wait_recv()
     stencil(0, 0)
     p1_down.start()
-    lax.fori_loop(1, rows, stencil, 0)
+    stencil(rows - 1, 0)
 
     @pl.when(has_down)
     def _():
         p2_down.start()
-
-    out_t = pltpu.make_async_copy(OT, out_thermal, osem.at[0])
-    out_t.start()
 
     @pl.when(has_up)
     def _():
@@ -530,17 +527,30 @@
 
     lax.fori_loop(1, ny, send_back, 0)
     B2[gy] = A2[gy]
-    wait_all(A2, B2, bs, br)
-
-    q = jnp.concatenate([B2[s] for s in range(ny)], 1)
-    high, low = split_rows(q)
-    S[0:half_rows, :] = high
-    S[half_rows:, :] = low
+
     width = length // chunks
-    for c in range(chunks):
-        wide = dot32(S[...], HH[c])
-        part = wide[:half_rows] + wide[half_rows:] + dot32(S[0:half_rows, :], HL[c])
-        PR[1 : rows + 1, :, c * width : (c + 1) * width] = part.reshape(rows, layers, width)
+    for i in range(chunks):
+        k = (gy // 2 + chunks - i) % chunks
+        for side in range(2):
+            peer = 2 * k + side
+
+            @pl.when(peer != gy)
+            def _():
+                remote(
+                    A2.at[peer], B2.at[peer], bs.at[peer], br.at[peer], peer, gz
+                ).wait_recv()
+
+        high, low = split_rows(jnp.concatenate([B2[2 * k], B2[2 * k + 1]], 1))
+        both = jnp.concatenate([high, low], 0)
+        span = pl.ds(pl.multiple_of(k * 256, 256), 256)
+        for c in range(chunks):
+            wide = dot32(both, HH[c, span, :])
+            part = wide[:half_rows] + wide[half_rows:] + dot32(high, HL[c, span, :])
+            part = part.reshape(rows, layers, width)
+            cols = slice(c * width, (c + 1) * width)
+            if i:
+                part = part + PR[1 : rows + 1, :, cols]
+            PR[1 : rows + 1, :, cols] = part
     pr_up = remote(PR.at[rows], PR.at[0], hs.at[6], hr.at[6], up_y, gz)
     pz_up = remote(QZS, QZR, hs.at[7], hr.at[7], gy, gz + 1)
     pr_up.start()
@@ -571,8 +581,6 @@
         return carry
 
     lax.fori_loop(0, rows, project, 0)
-    out_m = pltpu.make_async_copy(OM, out_motion, osem.at[1])
-    out_m.start()
 
     @pl.when(has_down)
     def _():
@@ -597,8 +605,6 @@
     for i in range(1, nz):
         peer = (gz + i) % nz
         remote(MSG.at[0], MR.at[gz], zs.at[peer], zr.at[gz], gy, peer).wait_send()
-    out_t.wait()
-    out_m.wait()
 
 
 def fused_step(ny, nz, motion, thermal, flow, base):
@@ -637,10 +643,7 @@
         vmem((rows + 1, layers, length), f32),
         vmem((rows, length), f32),
         vmem((rows, length), f32),
-        vmem((3, rows, layers, length), f32),
-        vmem((rows, layers, length), f32),
         dma((9,)),
-        dma((2,)),
         dma((8,)),
         dma((8,)),
         dma((ny,)),
@@ -650,7 +653,8 @@
         dma((nz,)),
         dma((nz,)),
     ]
-    hbm = pl.BlockSpec(memory_space=pl.ANY)
+    hbm = pl.BlockSpec(memory_space=pltpu.HBM)
+    local = pl.BlockSpec(memory_space=pltpu.VMEM)
     return pl.pallas_call(
         functools.partial(fused_kernel, ny, nz),
         out_shape=(
@@ -658,10 +662,10 @@
             jax.ShapeDtypeStruct(thermal.shape, f32),
         ),
         in_specs=[hbm] * 9,
-        out_specs=(hbm, hbm),
+        out_specs=(local, local),
         scratch_shapes=scratch,
         compiler_params=pltpu.CompilerParams(
-            collective_id=0, has_side_effects=True, vmem_limit_bytes=44 * 2**20
+            collective_id=0, has_side_effects=True, vmem_limit_bytes=62 * 2**20
         ),
         cost_estimate=pl.CostEstimate(
             flops=12 * flat * length * length, bytes_accessed=10 * 2**20, transcendentals=0

time: 59.6 us -> 49.7 us (0.83)
  local copies, waits for them, and re-layouts: 12.2 us -> 3.58 us
  Pallas kernels: 46.3 us -> 45.3 us
    unnamed x20 -> x4, local copies, waits for them, and re-layouts: 12.2 us -> 3.58 us
    pallas_call x1, Pallas kernels: 46.3 us -> 45.3 us  [fused_step(): pl.pallas_call(functools.partial(fused_kernel, ny, nz), out_shape=(jax.Sh...]
where the time goes in v1:
time: 49.7 us; the launch traced here: 49.5 us
  Pallas kernels  45.3 us (91%)
  local copies, waits for them, and re-layouts  3.58 us (7%)
  between operations  0.65 us (1%)
    pallas_call x1, Pallas kernels, fused_step(): pl.pallas_call(functools.partial(fused_kernel, ny, nz), out_shape=(jax.Sh...  45.3 us
    unnamed x4, local copies, waits for them, and re-layouts  3.58 us

profile of v1, /device:TPU:0, one launch (start us, length us, event | category | flops | bytes accessed | tf_op | source)
XLA Modules:
  0.0 49.5 jit_solution(7473727515294702753)
XLA Ops:
  0.6 45.3 %shard_map.104 = (f32[3,8,16,1024]{3,2,1,0:T(8,128)}, f32[8,16,1024]{2,1,0:T(8,128)}) custom-call(f32[3,8,16,1024]{3,2,1,0:T(8,128)} %motion.1, f32[8,16,1024]{2,1,0:T(8,128)} %thermal.1, bf16[3,8,16,1024]{3,2,1,0:T(8,128)(2,1)} %flow.1, bf16[8,16,1024]{2,1,0:T(8,128)(2,1)} %base.1, bf16[4,1024,256]{2,1,0:T(8,128)(2,1)} %constant.10.clone.hx_hi, ...), custom_call_target="tpu_custom_call" | custom-call | flops 1610612736 | bytes 10485760 | tf_op jit(solution)/shard_map/pallas_call | solution.py:658
  45.9 0.0 copy-start
  45.9 2.8 %copy.13 = f32[3,8,16,1024]{3,2,1,0:T(8,128)} copy(f32[3,8,16,1024]{3,2,1,0:T(8,128)} %get-tuple-element.4) | data formatting | bytes 3145728
  48.7 0.0 copy-done
  48.7 0.8 %copy.14 = f32[8,16,1024]{2,1,0:T(8,128)} copy(f32[8,16,1024]{2,1,0:T(8,128)S(1)} %copy-done) | data formatting | bytes 1048576
Async XLA Ops:
  45.9 2.8 %copy-start = (f32[8,16,1024]{2,1,0:T(8,128)S(1)}, f32[8,16,1024]{2,1,0:T(8,128)}, u32[]{:S(2)}) copy-start(f32[8,16,1024]{2,1,0:T(8,128)} %get-tuple-element.5) | copy-start | bytes 1572868

commit v2 on v1

--- a/solution.py
+++ b/solution.py
@@ -248,9 +248,9 @@
 
 def fused_kernel(
     ny, nz, motion, thermal, flow, base, hx_hi, hx_lo, ty_in, modes_in, free_in,
-    OM, OT,
+    out_p, out_t, out_pr, out_z,
     F, U, TH, HH, HL, TY, LAM, FREE, ZS, ZR, P0, P1, P2, PZS, PZR, S, A, B, D, PHI,
-    R, MSG, MR, A2, B2, PR, QZS, QZR, lsem, hs, hr, as_, ar, bs, br, zs, zr,
+    R, MSG, MR, A2, B2, PR, QZS, QZR, OT, ZT, UZ, lsem, osem, ps, pr_, qs, qr, hs, hr, as_, ar, bs, br, zs, zr,
 ):
     gy, gz = lax.axis_index("gy"), lax.axis_index("gz")
     rows, layers, length = thermal.shape
@@ -341,6 +341,11 @@
     lax.fori_loop(0, nz, ratios, 0)
 
     loads[3].wait()
+    for y in range(rows):
+        for i, f in enumerate((2, 4)):
+            ZT[i, y : y + 1, :] = F[f, y + 1, 1:2, :]
+        for d in range(3):
+            UZ[d, y : y + 1, :] = U[d, y].astype(jnp.float32)[0:1, :]
 
     @pl.when(has_up)
     def _():
@@ -378,22 +383,43 @@
         c, t = advance(2)
         p2 = c + time_step * (t + half * (hzp - hzm))
         P2[y] = p2
-        PZS[pl.ds(y, 1), :] = p2[0:1, :]
         OT[y] = c3 + time_step * (t3 + buoyancy * c)
         return carry
 
     p1_down = remote(P1.at[0], P1.at[rows], hs.at[4], hr.at[4], down_y, gz)
     p2_down = remote(PZS, PZR, hs.at[5], hr.at[5], gy, gz - 1)
-    lax.fori_loop(1, rows - 1, stencil, 0)
+    inner = rows // 2
+    lax.fori_loop(1, inner, stencil, 0)
     y_down.wait_recv()
     y_up.wait_recv()
     stencil(0, 0)
     p1_down.start()
-    stencil(rows - 1, 0)
+
+    yi = lax.broadcasted_iota(jnp.int32, (rows, length), 0)
+    c = ZS[0, 2]
+    xp, xm = pltpu.roll(c, length - 1, 1), pltpu.roll(c, 1, 1)
+    yp = jnp.where(yi == rows - 1, F[2, rows + 1, 0:1, :], pltpu.roll(c, rows - 1, 0))
+    ym = jnp.where(yi == 0, F[2, 0, 0:1, :], pltpu.roll(c, 1, 0))
+    zp, zm = ZT[0], ZR[0, 2]
+    adv = 0.5 * (UZ[0] * (xp - xm) + UZ[1] * (yp - ym) + UZ[2] * (zp - zm))
+    lap = (xp + xm) + (yp + ym) + (zp + zm) - 6.0 * c
+    PZS[...] = c + time_step * (
+        adv + viscosity * lap + 0.5 * ZS[0, 3] * (ZT[1] - ZR[0, 4])
+    )
 
     @pl.when(has_down)
     def _():
         p2_down.start()
+
+    lax.fori_loop(inner, rows, stencil, 0)
+    outs = [
+        pltpu.make_async_copy(OT, out_t, osem.at[0]),
+        pltpu.make_async_copy(P0, out_p.at[0], osem.at[1]),
+        pltpu.make_async_copy(P1.at[0:rows], out_p.at[1], osem.at[2]),
+        pltpu.make_async_copy(P2, out_p.at[2], osem.at[3]),
+    ]
+    for copy in outs:
+        copy.start()
 
     @pl.when(has_up)
     def _():
@@ -529,6 +555,16 @@
     B2[gy] = A2[gy]
 
     width = length // chunks
+
+    def edge(c):
+        cols = slice(c * width, (c + 1) * width)
+        return (
+            remote(
+                PR.at[rows, :, cols], PR.at[0, :, cols], ps.at[c], pr_.at[c], up_y, gz
+            ),
+            remote(QZS.at[:, cols], QZR.at[:, cols], qs.at[c], qr.at[c], gy, gz + 1),
+        )
+
     for i in range(chunks):
         k = (gy // 2 + chunks - i) % chunks
         for side in range(2):
@@ -551,36 +587,36 @@
             if i:
                 part = part + PR[1 : rows + 1, :, cols]
             PR[1 : rows + 1, :, cols] = part
-    pr_up = remote(PR.at[rows], PR.at[0], hs.at[6], hr.at[6], up_y, gz)
-    pz_up = remote(QZS, QZR, hs.at[7], hr.at[7], gy, gz + 1)
-    pr_up.start()
-    for y in range(rows):
-        QZS[y : y + 1, :] = PR[y + 1, layers - 1 : layers, :]
-
-    @pl.when(has_up)
-    def _():
-        pz_up.start()
+            if i == chunks - 1:
+                QZS[:, cols] = jnp.concatenate(
+                    [part[y, layers - 1 : layers, :] for y in range(rows)], 0
+                )
+                pr_up, pz_up = edge(c)
+                pr_up.start()
+
+                @pl.when(has_up)
+                def _():
+                    pz_up.start()
 
     @pl.when(gz == 0)
     def _():
         for y in range(rows):
             QZR[y : y + 1, :] = PR[y + 1, 0:1, :]
 
-    @pl.when(has_down)
-    def _():
-        pz_up.wait_recv()
-
-    pr_up.wait_recv()
-
-    def project(y, carry):
-        p = PR[y + 1]
-        zm = jnp.where(zi == 0, QZR[pl.ds(y, 1), :], pltpu.roll(p, 1, 0))
-        OM[0, y] = P0[y] - (p - pltpu.roll(p, 1, 1))
-        OM[1, y] = P1[y] - (p - PR[y])
-        OM[2, y] = P2[y] - (p - zm)
-        return carry
-
-    lax.fori_loop(0, rows, project, 0)
+    for c in range(chunks):
+        pr_up, pz_up = edge(c)
+        pr_up.wait_recv()
+
+        @pl.when(has_down)
+        def _():
+            pz_up.wait_recv()
+
+    last = [
+        pltpu.make_async_copy(PR, out_pr, osem.at[4]),
+        pltpu.make_async_copy(QZR, out_z, osem.at[5]),
+    ]
+    for copy in last:
+        copy.start()
 
     @pl.when(has_down)
     def _():
@@ -590,9 +626,12 @@
     @pl.when(has_up)
     def _():
         z_up.wait_send()
-        pz_up.wait_send()
-
-    for copy in (y_down, y_up, p1_down, pr_up):
+        for c in range(chunks):
+            edge(c)[1].wait_send()
+
+    for c in range(chunks):
+        edge(c)[0].wait_send()
+    for copy in (y_down, y_up, p1_down):
         copy.wait_send()
 
     def finish(i, carry):
@@ -605,6 +644,21 @@
     for i in range(1, nz):
         peer = (gz + i) % nz
         remote(MSG.at[0], MR.at[gz], zs.at[peer], zr.at[gz], gy, peer).wait_send()
+    for copy in outs + last:
+        copy.wait()
+
+
+def project_kernel(prov, pressure, lower, thermal, out_motion, out_thermal):
+    _, count, layers, length = prov.shape
+    first = pl.program_id(0) * count
+    zi = lax.broadcasted_iota(jnp.int32, (layers, length), 0)
+    for y in range(count):
+        p = pressure[first + y + 1]
+        zm = jnp.where(zi == 0, lower[pl.ds(first + y, 1), :], pltpu.roll(p, 1, 0))
+        out_motion[0, y] = prov[0, y] - (p - pltpu.roll(p, 1, 1))
+        out_motion[1, y] = prov[1, y] - (p - pressure[first + y])
+        out_motion[2, y] = prov[2, y] - (p - zm)
+    out_thermal[...] = thermal[...]
 
 
 def fused_step(ny, nz, motion, thermal, flow, base):
@@ -643,9 +697,17 @@
         vmem((rows + 1, layers, length), f32),
         vmem((rows, length), f32),
         vmem((rows, length), f32),
+        vmem((rows, layers, length), f32),
+        vmem((2, rows, length), f32),
+        vmem((3, rows, length), f32),
         dma((9,)),
-        dma((8,)),
-        dma((8,)),
+        dma((6,)),
+        dma((ny // 2,)),
+        dma((ny // 2,)),
+        dma((ny // 2,)),
+        dma((ny // 2,)),
+        dma((6,)),
+        dma((6,)),
         dma((ny,)),
         dma((ny,)),
         dma((ny,)),
@@ -654,15 +716,16 @@
         dma((nz,)),
     ]
     hbm = pl.BlockSpec(memory_space=pltpu.HBM)
-    local = pl.BlockSpec(memory_space=pltpu.VMEM)
-    return pl.pallas_call(
+    prov, advanced, pressure, lower = pl.pallas_call(
         functools.partial(fused_kernel, ny, nz),
         out_shape=(
             jax.ShapeDtypeStruct(motion.shape, f32),
             jax.ShapeDtypeStruct(thermal.shape, f32),
+            jax.ShapeDtypeStruct((rows + 1, layers, length), f32),
+            jax.ShapeDtypeStruct((rows, length), f32),
         ),
         in_specs=[hbm] * 9,
-        out_specs=(local, local),
+        out_specs=(hbm,) * 4,
         scratch_shapes=scratch,
         compiler_params=pltpu.CompilerParams(
             collective_id=0, has_side_effects=True, vmem_limit_bytes=62 * 2**20
@@ -671,6 +734,25 @@
             flops=12 * flat * length * length, bytes_accessed=10 * 2**20, transcendentals=0
         ),
     )(motion, thermal, flow, base, *constants)
+    count = rows // 4
+    fields = pl.BlockSpec((3, count, layers, length), lambda i: (0, i, 0, 0))
+    single = pl.BlockSpec((count, layers, length), lambda i: (i, 0, 0))
+    return pl.pallas_call(
+        project_kernel,
+        grid=(4,),
+        out_shape=(
+            jax.ShapeDtypeStruct(motion.shape, f32),
+            jax.ShapeDtypeStruct(thermal.shape, f32),
+        ),
+        in_specs=[
+            fields,
+            pl.BlockSpec((rows + 1, layers, length), lambda i: (0, 0, 0)),
+            pl.BlockSpec((rows, length), lambda i: (0, 0)),
+            single,
+        ],
+        out_specs=(fields, single),
+        compiler_params=pltpu.CompilerParams(vmem_limit_bytes=62 * 2**20),
+    )(prov, pressure, lower, advanced)
 
 
 def solution(mesh):

time: 49.7 us -> 49.5 us (level)
  local copies, waits for them, and re-layouts: 3.58 us -> 0 us
  Pallas kernels: 45.3 us -> 48.7 us
    pallas_call x0 -> x1, Pallas kernels: none -> 4.14 us  [fused_step(): pl.pallas_call(project_kernel, grid=(4,), out_shape=(jax.ShapeDtypeStruct...]
    unnamed x4 -> x0, local copies, waits for them, and re-layouts: 3.58 us -> none
    pallas_call x1, Pallas kernels: 45.3 us -> 44.6 us  [fused_step(): pl.pallas_call(functools.partial(fused_kernel, ny, nz), out_shape=(jax.Sh...]
where the time goes in v2:
time: 49.5 us; the launch traced here: 49.3 us
  Pallas kernels  48.7 us (98%)
  between operations  0.64 us (1%)
    pallas_call x1, Pallas kernels, fused_step(): pl.pallas_call(functools.partial(fused_kernel, ny, nz), out_shape=(jax.Sh...  44.6 us
    pallas_call x1, Pallas kernels, fused_step(): pl.pallas_call(project_kernel, grid=(4,), out_shape=(jax.ShapeDtypeStruct...  4.14 us

profile of v2, /device:TPU:0, one launch (start us, length us, event | category | flops | bytes accessed | tf_op | source)
XLA Modules:
  0.0 49.3 jit_solution(13426503747432601727)
XLA Ops:
  0.6 44.6 %shard_map.104 = (f32[3,8,16,1024]{3,2,1,0:T(8,128)}, f32[8,16,1024]{2,1,0:T(8,128)}, f32[9,16,1024]{2,1,0:T(8,128)}, f32[8,1024]{1,0:T(8,128)}) custom-call(f32[3,8,16,1024]{3,2,1,0:T(8,128)} %motion.1, f32[8,16,1024]{2,1,0:T(8,128)} %thermal.1, bf16[3,8,16,1024]{3,2,1,0:T(8,128)(2,1)} %flow.1, bf16[8,16,1024]{2,1,0:T(8,128)(2,1)} %base.1, ...), custom_call_target="tpu_custom_call" | custom-call | flops 1610612736 | bytes 10485760 | tf_op jit(solution)/shard_map/pallas_call | solution.py:719
  45.2 4.1 %shard_map.105 = (f32[3,8,16,1024]{3,2,1,0:T(8,128)}, f32[8,16,1024]{2,1,0:T(8,128)}) custom-call(f32[3,8,16,1024]{3,2,1,0:T(8,128)} %get-tuple-element.6.prov, f32[9,16,1024]{2,1,0:T(8,128)} %get-tuple-element.7.pressure, f32[8,1024]{1,0:T(8,128)} %get-tuple-element.8.lower, f32[8,16,1024]{2,1,0:T(8,128)} %get-tuple-element.9.thermal), custom_call_target="tpu_custom_call" | custom-call | tf_op jit(solution)/shard_map/pallas_call | solution.py:740

commit v3 on v2

--- a/solution.py
+++ b/solution.py
@@ -388,7 +388,7 @@
 
     p1_down = remote(P1.at[0], P1.at[rows], hs.at[4], hr.at[4], down_y, gz)
     p2_down = remote(PZS, PZR, hs.at[5], hr.at[5], gy, gz - 1)
-    inner = rows // 2
+    inner = rows - 2
     lax.fori_loop(1, inner, stencil, 0)
     y_down.wait_recv()
     y_up.wait_recv()
@@ -734,12 +734,12 @@
             flops=12 * flat * length * length, bytes_accessed=10 * 2**20, transcendentals=0
         ),
     )(motion, thermal, flow, base, *constants)
-    count = rows // 4
+    count = rows // 2
     fields = pl.BlockSpec((3, count, layers, length), lambda i: (0, i, 0, 0))
     single = pl.BlockSpec((count, layers, length), lambda i: (i, 0, 0))
     return pl.pallas_call(
         project_kernel,
-        grid=(4,),
+        grid=(2,),
         out_shape=(
             jax.ShapeDtypeStruct(motion.shape, f32),
             jax.ShapeDtypeStruct(thermal.shape, f32),

time: 49.5 us -> 47.9 us (0.968)
  Pallas kernels: 48.7 us -> 47.1 us
    pallas_call x1, Pallas kernels: 4.14 us -> 2.88 us  [fused_step(): pl.pallas_call(project_kernel, grid=(2,), out_shape=(jax.ShapeDtypeStruct...]
where the time goes in v3:
time: 47.9 us; the launch traced here: 47.8 us
  Pallas kernels  47.1 us (98%)
  between operations  0.64 us (1%)
    pallas_call x1, Pallas kernels, fused_step(): pl.pallas_call(functools.partial(fused_kernel, ny, nz), out_shape=(jax.Sh...  44.3 us
    pallas_call x1, Pallas kernels, fused_step(): pl.pallas_call(project_kernel, grid=(2,), out_shape=(jax.ShapeDtypeStruct...  2.88 us

profile of v3, /device:TPU:0, one launch (start us, length us, event | category | flops | bytes accessed | tf_op | source)
XLA Modules:
  0.0 47.8 jit_solution(6466858787419953731)
XLA Ops:
  0.6 44.3 %shard_map.104 = (f32[3,8,16,1024]{3,2,1,0:T(8,128)}, f32[8,16,1024]{2,1,0:T(8,128)}, f32[9,16,1024]{2,1,0:T(8,128)}, f32[8,1024]{1,0:T(8,128)}) custom-call(f32[3,8,16,1024]{3,2,1,0:T(8,128)} %motion.1, f32[8,16,1024]{2,1,0:T(8,128)} %thermal.1, bf16[3,8,16,1024]{3,2,1,0:T(8,128)(2,1)} %flow.1, bf16[8,16,1024]{2,1,0:T(8,128)(2,1)} %base.1, ...), custom_call_target="tpu_custom_call" | custom-call | flops 1610612736 | bytes 10485760 | tf_op jit(solution)/shard_map/pallas_call | solution.py:719
  44.9 2.9 %shard_map.105 = (f32[3,8,16,1024]{3,2,1,0:T(8,128)}, f32[8,16,1024]{2,1,0:T(8,128)}) custom-call(f32[3,8,16,1024]{3,2,1,0:T(8,128)} %get-tuple-element.6.prov, f32[9,16,1024]{2,1,0:T(8,128)} %get-tuple-element.7.pressure, f32[8,1024]{1,0:T(8,128)} %get-tuple-element.8.lower, f32[8,16,1024]{2,1,0:T(8,128)} %get-tuple-element.9.thermal), custom_call_target="tpu_custom_call" | custom-call | tf_op jit(solution)/shard_map/pallas_call | solution.py:740
